TPU v7x, 32 devices: a whole 2x2x4 slice. The times are simulated.
32 devices in a mesh: sample: 4 (over y, x), row: 2 (over core), col: 4 (over z).
Axes of the slice: x: 2, y: 2, z: 4, core: 2. Of those that a mesh axis runs over, the one named last changes fastest.
Arguments:
- pair: bfloat16 [896, 224, 128], P(('sample', 'row'), 'col'), parts along dimension 0, may hold values from -6 to 6
- pair_gain: float32 [128], replicated, may hold values from 0.1 to 1.9
- bias_weight: bfloat16 [128, 16], replicated, may hold values from -0.5 to 0.5
- single: bfloat16 [896, 384], P(('sample', 'row', 'col')), parts along dimension 0, may hold values from -50 to 50
- w_query: bfloat16 [384, 384], replicated, may hold values from -0.30618622 to 0.30618622
- w_key: bfloat16 [384, 384], replicated, may hold values from -0.30618622 to 0.30618622
- w_value: bfloat16 [384, 384], replicated, may hold values from -0.3125 to 0.3125
- w_out: bfloat16 [384, 384], replicated, may hold values from -0.3125 to 0.3125
- key_mask: int32 [896], P(('sample', 'col')), parts along dimension 0, may hold values from 0 to 1, as said below
- out_grad: bfloat16 [896, 384], P(('sample', 'row', 'col')), parts along dimension 0, may hold values from -6 to 6
Outputs:
- pair_grad: bfloat16 [896, 224, 128], P(('sample', 'row'), 'col'), parts along dimension 0
- single_grad: bfloat16 [896, 384], P(('sample', 'row', 'col')), parts along dimension 0
- query_weight_grad: float32 [1536, 384], P(('sample', 'row', 'col')), parts along dimension 0
- key_weight_grad: float32 [1536, 384], P(('sample', 'row', 'col')), parts along dimension 0
- value_weight_grad: float32 [1536, 384], P(('sample', 'row', 'col')), parts along dimension 0
- out_weight_grad: float32 [1536, 384], P(('sample', 'row', 'col')), parts along dimension 0
- bias_weight_grad: float32 [512, 16], P('sample'), parts along dimension 0
- gain_grad: float32 [512], P('sample'), parts along dimension 0
There are 4 independent parts, one for each index of `sample`. A program takes and returns all parts, laid end to end along the dimension named above; an argument that names none is the same for every part. Nothing has to cross between parts.
Inputs may be any that keep to these rules, and one draw needn't show every extreme that they name: key_mask is 1 exactly on a prefix of the tokens whose length is a multiple of 4, at least half of 224 and at most 220, and 0 after it.
All inputs are finite; a program needn't handle non-finite values.
Results may differ from a plain program's by a relative error of at most 0.04.
Values may be sent and summed in bfloat16 or wider, within the bound.
A program may use at most 64 MiB of HBM per device.

v0:
```python
import jax
import jax.numpy as jnp
from jax import lax
from jax.sharding import PartitionSpec as P

HEADS = 16
HEAD = 24


norm_eps = 1e-05
masked_score = -1000000000.0
highest = lax.Precision.HIGHEST


def project(grads, weight):
    return jnp.dot(grads, weight.astype(jnp.float32).T, precision=highest)


def transposed_product(left, right):
    return jnp.einsum("te,td->ed", left.astype(jnp.float32), right, precision=highest)


def body(pair, pair_gain, bias_weight, single, w_query, w_key, w_value, w_out, key_mask, out_grad):
    f32 = jnp.float32
    bf16 = jnp.bfloat16
    row_count = pair.shape[0]
    col_count = pair.shape[1]
    own_count = single.shape[0]
    model_width = single.shape[1]
    row_index = lax.axis_index("row")
    col_index = lax.axis_index("col")
    score_scale = HEAD ** (-0.5)
    all_single = lax.all_gather(single, ("row", "col"), axis=0, tiled=True)
    single_rows = lax.dynamic_slice_in_dim(all_single, row_index * row_count, row_count, 0)
    single_cols = lax.dynamic_slice_in_dim(all_single, col_index * col_count, col_count, 0)
    grad_rows = lax.all_gather(out_grad, "col", axis=0, tiled=True)
    query_rows = jnp.dot(single_rows, w_query, preferred_element_type=f32).astype(bf16)
    key_cols = jnp.dot(single_cols, w_key, preferred_element_type=f32).astype(bf16)
    value_cols = jnp.dot(single_cols, w_value, preferred_element_type=f32).astype(bf16)
    pair_float = pair.astype(f32)
    centred = pair_float - jnp.mean(pair_float, axis=2, keepdims=True)
    inverse = lax.rsqrt(jnp.mean(centred * centred, axis=2, keepdims=True) + norm_eps)
    normed = centred * inverse
    pair_normed = (normed * pair_gain).astype(bf16)
    pair_bias = jnp.einsum("ijc,ch->hij", pair_normed, bias_weight, preferred_element_type=f32)
    query_heads = query_rows.reshape(row_count, HEADS, HEAD)
    key_heads = key_cols.reshape(col_count, HEADS, HEAD)
    value_heads = value_cols.reshape(col_count, HEADS, HEAD)
    scores = (
        jnp.einsum("ihd,jhd->hij", query_heads, key_heads, preferred_element_type=f32) * score_scale
        + pair_bias
    )
    scores = jnp.where(key_mask[None, None, :] > 0, scores, masked_score)
    local_top = jnp.max(scores, axis=2)
    row_top = lax.pmax(local_top, "col")
    exp_scores = jnp.exp(scores - row_top[:, :, None])
    row_total = lax.psum(jnp.sum(exp_scores, axis=2), "col")
    probs = exp_scores / row_total[:, :, None]
    probs_low = probs.astype(bf16)
    attended_part = jnp.einsum(
        "hij,jhd->ihd", probs_low, value_heads, preferred_element_type=f32
    ).reshape(row_count, model_width)
    attended = lax.psum(attended_part, "col")
    attended_low = attended.astype(bf16)
    grad_att = jnp.dot(grad_rows, w_out.T, preferred_element_type=f32).astype(bf16)
    grad_heads = grad_att.reshape(row_count, HEADS, HEAD)
    grad_probs = jnp.einsum("ihd,jhd->hij", grad_heads, value_heads, preferred_element_type=f32)
    row_delta = jnp.einsum(
        "ihd,ihd->hi", grad_heads.astype(f32), attended.reshape(row_count, HEADS, HEAD)
    )
    grad_scores = probs * (grad_probs - row_delta[:, :, None])
    grad_low = grad_scores.astype(bf16)
    query_grad = (
        jnp.einsum("hij,jhd->ihd", grad_low, key_heads, preferred_element_type=f32) * score_scale
    ).reshape(row_count, model_width)
    key_grad = (
        jnp.einsum("hij,ihd->jhd", grad_low, query_heads, preferred_element_type=f32) * score_scale
    ).reshape(col_count, model_width)
    value_grad = jnp.einsum(
        "hij,ihd->jhd", probs_low, grad_heads, preferred_element_type=f32
    ).reshape(col_count, model_width)
    grad_normed = jnp.einsum("hij,ch->ijc", grad_low, bias_weight, preferred_element_type=f32)
    bias_grad_part = jnp.einsum("ijc,hij->ch", pair_normed, grad_low, preferred_element_type=f32)
    gain_grad_part = jnp.sum(grad_normed * normed, axis=(0, 1))
    bias_weight_grad, gain_grad = lax.psum((bias_grad_part, gain_grad_part), ("row", "col"))
    scaled = grad_normed * pair_gain
    pair_grad = (
        inverse
        * (
            scaled
            - jnp.mean(scaled, axis=2, keepdims=True)
            - normed * jnp.mean(scaled * normed, axis=2, keepdims=True)
        )
    ).astype(bf16)
    own_start = col_index * own_count
    term_full = jnp.zeros((all_single.shape[0], model_width), f32)
    term_full = lax.dynamic_update_slice_in_dim(
        term_full, project(query_grad, w_query), row_index * row_count, 0
    )
    key_side = project(key_grad, w_key) + project(value_grad, w_value)
    current = lax.dynamic_slice_in_dim(term_full, col_index * col_count, col_count, 0)
    term_full = lax.dynamic_update_slice_in_dim(
        term_full, current + key_side, col_index * col_count, 0
    )
    single_grad = lax.psum_scatter(
        term_full, ("row", "col"), scatter_dimension=0, tiled=True
    ).astype(bf16)
    own_att = lax.dynamic_slice_in_dim(attended_low, own_start, own_count, 0)
    out_terms = jnp.einsum("te,td->ed", own_att, out_grad, preferred_element_type=f32)
    weight_sums = (
        lax.psum_scatter(
            transposed_product(single_rows, query_grad),
            ("row", "col"),
            scatter_dimension=0,
            tiled=True,
        ),
        lax.psum_scatter(
            transposed_product(single_cols, key_grad),
            ("row", "col"),
            scatter_dimension=0,
            tiled=True,
        ),
        lax.psum_scatter(
            transposed_product(single_cols, value_grad),
            ("row", "col"),
            scatter_dimension=0,
            tiled=True,
        ),
        lax.psum_scatter(out_terms, ("row", "col"), scatter_dimension=0, tiled=True),
    )
    query_weight_grad, key_weight_grad, value_weight_grad, out_weight_grad = weight_sums
    return (
        pair_grad,
        single_grad,
        query_weight_grad,
        key_weight_grad,
        value_weight_grad,
        out_weight_grad,
        bias_weight_grad,
        gain_grad,
    )


def solution(mesh):
    in_specs = (
        P(("sample", "row"), "col", None),
        P(),
        P(),
        P(("sample", "row", "col"), None),
        P(),
        P(),
        P(),
        P(),
        P(("sample", "col")),
        P(("sample", "row", "col"), None),
    )
    out_specs = (
        P(("sample", "row"), "col", None),
        P(("sample", "row", "col"), None),
        P(("sample", "row", "col"), None),
        P(("sample", "row", "col"), None),
        P(("sample", "row", "col"), None),
        P(("sample", "row", "col"), None),
        P("sample", None),
        P("sample"),
    )
    return jax.shard_map(body, mesh=mesh, in_specs=in_specs, out_specs=out_specs, check_vma=False)
```

profile of v0, /device:TPU:0, one launch (start us, length us, event | category | flops | bytes accessed | tf_op | source)
XLA Modules:
  0.0 231.9 jit_solution(12683231622605221813)
XLA Ops:
  8.1 0.8 broadcast_compare_fusion
  8.9 2.3 %convert_reduce_fusion = f32[112,56]{1,0:T(8,128)S(1)} fusion(bf16[112,56,128]{2,1,0:T(8,128)(2,1)} %param.10), kind=kLoop, calls=%fused_computation.1 | loop fusion | flops 1599360 | bytes 1630720 | tf_op jit(solution)/shard_map/reduce_sum | solution.py:41
  11.3 3.0 %fusion.13 = f32[112,56]{1,0:T(8,128)S(1)} fusion(bf16[112,56,128]{2,1,0:T(8,128)(2,1)} %param.10, f32[112,56]{1,0:T(8,128)S(1)} %broadcast_multiply_fusion.2), kind=kLoop, calls=%fused_computation.14 | loop fusion | flops 3204992 | bytes 1655808 | tf_op jit(solution)/shard_map/reduce_sum | solution.py:42
  14.3 26.3 %all-gather = bf16[8,28,384]{2,1,0:T(8,128)(2,1)S(1)} all-gather(bf16[1,28,384]{2,1,0:T(8,128)(2,1)S(1)} %bitcast.86), channel_id=1, replica_groups=mesh['sample'=4,'row'=2,'col'=4] {'row','col'}, dimensions={0}, use_global_device_ids=true | all-gather | bytes 193536 | tf_op jit(solution)/shard_map/all_gather | solution.py:33
  41.2 0.7 copy.42
  42.3 3.3 %fusion.21 = f32[112,56,16]{1,2,0:T(8,128)} fusion(bf16[112,56,128]{2,1,0:T(8,128)(2,1)S(1)} %copy-done.1, f32[128]{0:T(128)S(1)} %copy-done.12, f32[112,56]{1,0:T(8,128)S(1)} %add_rsqrt_fusion, f32[112,56]{1,0:T(8,128)S(1)} %broadcast_multiply_fusion.2, bf16[128,16]{0,1:T(8,128)(2,1)S(1)} %copy-done.14), kind=kOutput, calls=%fused_computation.33 | convolution fusion | flops 29704192 | bytes 2061824 | tf_op jit(solution)/shard_map/ijc,ch->hij/dot_general | solution.py:45
  45.6 1.5 copy.40
  47.5 11.8 %pmax.7 = f32[16,112]{1,0:T(8,128)S(1)} all-reduce(f32[16,112]{1,0:T(8,128)S(1)} %get-tuple-element.13), channel_id=1, replica_groups=mesh['sample'=4,'row'=2,'col'=4] {'col'}, use_global_device_ids=true, to_apply=%region_3.4 | all-reduce | flops 1792 | bytes 14336 | tf_op jit(solution)/shard_map/pmax | solution.py:55
  59.4 8.6 %psum.28 = f32[16,112]{1,0:T(8,128)S(1)} all-reduce(f32[16,112]{1,0:T(8,128)S(1)} %fusion.24), channel_id=1, replica_groups=mesh['sample'=4,'row'=2,'col'=4] {'col'}, use_global_device_ids=true, to_apply=%region_5.6 | all-reduce | flops 1792 | bytes 14336 | tf_op jit(solution)/shard_map/psum | solution.py:57
  68.1 1.8 fusion.48
  70.0 13.4 %all-gather.1 = bf16[4,28,384]{2,1,0:T(8,128)(2,1)S(1)} all-gather(bf16[1,28,384]{2,1,0:T(8,128)(2,1)} %bitcast.85), channel_id=1, replica_groups=mesh['sample'=4,'row'=2,'col'=4] {'col'}, dimensions={0}, use_global_device_ids=true | all-gather | bytes 107520 | tf_op jit(solution)/shard_map/all_gather | solution.py:36
  83.5 1.2 convolution_convert_fusion
  85.0 1.3 fusion.31
  86.4 18.8 %all-reduce.5.cloned.1.call-done = f32[112,384]{0,1:T(8,128)} async-done(((f32[112,384]{0,1:T(8,128)}), f32[112,384]{0,1:T(8,128)}) %all-reduce.5.cloned.1.call-update) | async-done | bytes 172048 | tf_op jit(solution)/shard_map/psum | solution.py:63
  105.2 1.0 fusion.25
  106.2 1.2 fusion.17
  107.7 1.3 fusion.28
  109.0 1.2 dynamic-slice.4
  110.9 1.1 convolution_multiply_fusion.1
  112.0 1.3 fusion.33
  113.4 0.5 fusion.49
  113.9 1.1 copy.43
  116.1 21.5 %fusion = f32[32,384]{1,0:T(8,128)S(1)} fusion(f32[224,384]{1,0:T(8,128)S(1)} %fusion.19), kind=kCustom, calls=%all-reduce-scatter | all-reduce-scatter fusion | flops 98305 | bytes 393728
  137.7 4.0 %collective-permute-start = (bf16[28,384]{1,0:T(8,128)(2,1)S(1)}, bf16[28,384]{1,0:T(8,128)(2,1)S(1)}, u32[]{:S(2)}, u32[]{:S(2)}) collective-permute-start(bf16[28,384]{1,0:T(8,128)(2,1)S(1)} %slice), channel_id=1, source_target_pairs={{0,1},{1,2},{2,3},{3,4},{4,5},{5,6},{6,7},{8,9},{9,10},{10,11},{11... | collective-permute-start | bytes 64520
  141.7 2.1 fusion.27
  143.8 5.3 %fusion.12 = (f32[128]{0:T(128)S(1)}, f32[112,56]{1,0:T(8,128)S(1)}, f32[112,56]{1,0:T(8,128)S(1)}, f32[112,56,128]{2,1,0:T(8,128)S(1)}) fusion(bf16[112,56,128]{2,1,0:T(8,128)(2,1)S(1)} %copy-done.1, f32[112,56]{1,0:T(8,128)} %copy-done.9, f32[112,56]{1,0:T(8,128)S(1)} %broadcast_multiply_fusion.2, f32[128]{0:T(128)S(1)} %copy-done.13, ...), kind=kOutput, calls=%fused_computation.13 | convolution fusion | flops 32902784 | bytes 5123072 | tf_op jit(solution)/shard_map/hij,ch->ijc/dot_general | solution.py:82
  149.1 5.2 %fusion.11 = bf16[112,56,128]{2,1,0:T(8,128)(2,1)} fusion(bf16[112,56,128]{2,1,0:T(8,128)(2,1)S(1)} %copy-done.1, f32[112,56,128]{2,1,0:T(8,128)S(1)} %get-tuple-element.15, f32[112,56]{1,0:T(8,128)S(1)} %get-tuple-element.16, f32[112,56]{1,0:T(8,128)S(1)} %get-tuple-element.17, f32[128]{0:T(128)S(1)} %copy-done.13, f32[112,56]{1,0:T(8,128)S(1)} %copy-done.10, ...), kind=kLoop, calls=%fused_computation.12 | loop fusion | flops 7225344 | bytes 6523392 | tf_op jit(solution)/shard_map/convert_element_type | solution.py:94
  154.3 2.0 convolution_bitcast_fusion
  156.3 16.5 %all-reduce.2 = (f32[128,16]{0,1:T(8,128)}, f32[128]{0:T(128)}) all-reduce(f32[128,16]{0,1:T(8,128)S(1)} %convolution_bitcast_fusion, f32[128]{0:T(128)S(1)} %get-tuple-element.8), channel_id=1, replica_groups=mesh['sample'=4,'row'=2,'col'=4] {'row','col'}, use_global_device_ids=true, to_apply=%region_14.15 | all-reduce | flops 2176 | bytes 17408 | tf_op jit(solution)/shard_map/psum | solution.py:85
  173.0 0.6 dynamic-slice_convert_fusion.2
  173.6 15.2 %reduce-scatter.9.cloned.1.call-done = f32[48,384]{1,0:T(8,128)} async-done(((f32[384,384]{1,0:T(8,128)}), f32[48,384]{1,0:T(8,128)}) %reduce-scatter.9.cloned.1.call-update) | async-done | bytes 73744 | tf_op jit(solution)/shard_map/reduce_scatter | solution.py:117
  188.8 35.5 %reduce-scatter.13.cloned.1.call-done = f32[48,384]{1,0:T(8,128)} async-done(((f32[384,384]{1,0:T(8,128)}), f32[48,384]{1,0:T(8,128)}) %reduce-scatter.13.cloned.1.call-update) | async-done | bytes 73744 | tf_op jit(solution)/shard_map/reduce_scatter | solution.py:129
  (66 shorter events, 3.6 us)
Async XLA Ops:
  8.0 33.9 %copy-start = (bf16[384,384]{1,0:T(8,128)(2,1)S(1)}, bf16[384,384]{1,0:T(8,128)(2,1)}, u32[]{:S(2)}) copy-start(bf16[384,384]{1,0:T(8,128)(2,1)} %param.14) | copy-start | bytes 884740
  8.0 34.2 %copy-start.1 = (bf16[112,56,128]{2,1,0:T(8,128)(2,1)S(1)}, bf16[112,56,128]{2,1,0:T(8,128)(2,1)}, u32[]{:S(2)}) copy-start(bf16[112,56,128]{2,1,0:T(8,128)(2,1)} %param.10) | copy-start | bytes 4816900
  8.0 6.3 %copy-start.11 = (bf16[28,384]{1,0:T(8,128)(2,1)S(1)}, bf16[28,384]{1,0:T(8,128)(2,1)}, u32[]{:S(2)}) copy-start(bf16[28,384]{1,0:T(8,128)(2,1)} %param.13) | copy-start | bytes 64516
  8.0 32.6 %copy-start.3 = (bf16[384,384]{1,0:T(8,128)(2,1)S(1)}, bf16[384,384]{1,0:T(8,128)(2,1)}, u32[]{:S(2)}) copy-start(bf16[384,384]{1,0:T(8,128)(2,1)} %param.16) | copy-start | bytes 884740
  8.0 32.8 %copy-start.2 = (bf16[384,384]{1,0:T(8,128)(2,1)S(1)}, bf16[384,384]{1,0:T(8,128)(2,1)}, u32[]{:S(2)}) copy-start(bf16[384,384]{1,0:T(8,128)(2,1)} %param.15) | copy-start | bytes 884740
  8.1 34.2 %copy-start.12 = (f32[128]{0:T(128)S(1)}, f32[128]{0:T(128)}, u32[]{:S(2)}) copy-start(f32[128]{0:T(128)} %param.11) | copy-start | bytes 1540
  8.1 34.2 %copy-start.14 = (bf16[128,16]{0,1:T(8,128)(2,1)S(1)}, bf16[128,16]{0,1:T(8,128)(2,1)}, u32[]{:S(2)}) copy-start(bf16[128,16]{0,1:T(8,128)(2,1)} %param.12) | copy-start | bytes 12292
  8.1 97.1 %all-reduce.5.cloned.1.call-start = ((), (), s32[]{:S(2)}) async-start(), calls=%async_computation.4 | async-start | bytes 393216 | tf_op jit(solution)/shard_map/psum | solution.py:63
  14.3 32.8 %copy-start.9 = (f32[112,56]{1,0:T(8,128)}, f32[112,56]{1,0:T(8,128)S(1)}, u32[]{:S(2)}) copy-start(f32[112,56]{1,0:T(8,128)S(1)} %add_rsqrt_fusion) | copy-start | bytes 75268
  41.2 6.3 %copy-start.6 = (bf16[56,384]{0,1:T(8,128)(2,1)}, bf16[56,384]{0,1:T(8,128)(2,1)S(1)}, u32[]{:S(2)}) copy-start(bf16[56,384]{0,1:T(8,128)(2,1)S(1)} %copy.39) | copy-start | bytes 129028
  42.3 17.1 %copy-start.5 = (bf16[112,384]{0,1:T(8,128)(2,1)}, bf16[112,384]{0,1:T(8,128)(2,1)S(1)}, u32[]{:S(2)}) copy-start(bf16[112,384]{0,1:T(8,128)(2,1)S(1)} %copy.38) | copy-start | bytes 258052
  68.1 39.3 %copy-start.7 = (bf16[56,384]{0,1:T(8,128)(2,1)S(1)}, bf16[56,384]{0,1:T(8,128)(2,1)}, u32[]{:S(2)}) copy-start(bf16[56,384]{0,1:T(8,128)(2,1)} %copy-done.6) | copy-start | bytes 129028
  69.9 103.6 %reduce-scatter.11.cloned.1.call-start = ((), (), s32[]{:S(2)}) async-start(), calls=%async_computation.7 | async-start | bytes 663552 | tf_op jit(solution)/shard_map/reduce_scatter | solution.py:123
  86.4 87.2 %reduce-scatter.7.cloned.1.call-start = ((), (), s32[]{:S(2)}) async-start(), calls=%async_computation.5 | async-start | bytes 663552 | tf_op jit(solution)/shard_map/reduce_scatter | solution.py:111
  107.4 8.2 %copy-start.4 = (bf16[384,384]{1,0:T(8,128)(2,1)S(1)}, bf16[384,384]{1,0:T(8,128)(2,1)}, u32[]{:S(2)}) copy-start(bf16[384,384]{1,0:T(8,128)(2,1)} %param.16) | copy-start | bytes 884740
  108.9 79.9 %reduce-scatter.9.cloned.1.call-start = ((), (), s32[]{:S(2)}) async-start(), calls=%async_computation.6 | async-start | bytes 663552 | tf_op jit(solution)/shard_map/reduce_scatter | solution.py:117
  112.0 31.8 %copy-start.13 = (f32[128]{0:T(128)S(1)}, f32[128]{0:T(128)}, u32[]{:S(2)}) copy-start(f32[128]{0:T(128)} %param.11) | copy-start | bytes 1540
  112.0 31.8 %copy-start.15 = (bf16[128,16]{0,1:T(8,128)(2,1)S(1)}, bf16[128,16]{0,1:T(8,128)(2,1)}, u32[]{:S(2)}) copy-start(bf16[128,16]{0,1:T(8,128)(2,1)} %param.12) | copy-start | bytes 12292
  113.4 110.9 %reduce-scatter.13.cloned.1.call-start = ((), (), s32[]{:S(2)}) async-start(), calls=%async_computation.8 | async-start | bytes 663552 | tf_op jit(solution)/shard_map/reduce_scatter | solution.py:129
  137.7 35.1 %collective-permute-start = (bf16[28,384]{1,0:T(8,128)(2,1)S(1)}, bf16[28,384]{1,0:T(8,128)(2,1)S(1)}, u32[]{:S(2)}, u32[]{:S(2)}) collective-permute-start(bf16[28,384]{1,0:T(8,128)(2,1)S(1)} %slice), channel_id=1, source_target_pairs={{0,1},{1,2},{2,3},{3,4},{4,5},{5,6},{6,7},{8,9},{9,10},{10,11},{11... | collective-permute-start | bytes 64520
  143.8 5.3 %copy-start.10 = (f32[112,56]{1,0:T(8,128)S(1)}, f32[112,56]{1,0:T(8,128)}, u32[]{:S(2)}) copy-start(f32[112,56]{1,0:T(8,128)} %copy-done.9) | copy-start | bytes 75268
  149.1 5.2 %copy-start.8 = (bf16[16,112,56]{2,0,1:T(8,128)(2,1)S(1)}, bf16[16,112,56]{2,0,1:T(8,128)(2,1)}, u32[]{:S(2)}) copy-start(bf16[16,112,56]{2,0,1:T(8,128)(2,1)} %copy.43) | copy-start | bytes 602116
Sparse Core Ops, SparseCore 0:
  70.1 35.1 all-reduce.4
Sparse Core Ops, SparseCore 1:
  86.4 32.5 reduce-scatter.10
  121.8 32.8 reduce-scatter.6
  157.5 31.2 reduce-scatter.8
  191.8 32.5 reduce-scatter.12
where the time goes:
time: 232 us
  blocking collectives  98.1 us (42%)
  waiting for transfers between devices  69.6 us (30%)
  matrix products  24.6 us (11%)
  between operations  16.8 us (7%)
  other arithmetic  12.5 us (5%)
  local copies, waits for them, and re-layouts  6.04 us (3%)
  starting transfers between devices  4.23 us (2%)
    reduce_scatter x1, waiting for transfers between devices, body(): lax.psum_scatter(out_terms, ('row', 'col'), scatter_dimension=0, tiled=True)  35.5 us
    all_gather x1, blocking collectives, body(): all_single = lax.all_gather(single, ('row', 'col'), axis=0, tiled=True)  26.3 us
    unnamed x1, blocking collectives  21.5 us
    psum x1, waiting for transfers between devices, body(): attended = lax.psum(attended_part, 'col')  18.8 us
    psum x1, blocking collectives, body(): lax.psum((bias_grad_part, gain_grad_part), ('row', 'col'))  16.5 us
    reduce_scatter x1, waiting for transfers between devices, body(): lax.psum_scatter(transposed_product(single_cols, key_grad), ('row', 'col'...  15.2 us
    all_gather x1, blocking collectives, body(): grad_rows = lax.all_gather(out_grad, 'col', axis=0, tiled=True)  13.4 us
    pmax x1, blocking collectives, body(): row_top = lax.pmax(local_top, 'col')  11.8 us
  transfers between devices with their start and end apart: 6, of which 3 were waited for; matrix products, arithmetic and copies ran while one was open for 21% of the time, Pallas kernels for 0%

commit v1 on v0

v1 whole, which is shorter than its diff:
```python
import functools

import jax
import jax.numpy as jnp
from jax import lax
from jax.experimental import pallas as pl
from jax.experimental.pallas import tpu as pltpu
from jax.sharding import PartitionSpec as P

HEADS = 16
HEAD = 24

norm_eps = 1e-05
masked_score = -1000000000.0
f32 = jnp.float32
bf16 = jnp.bfloat16
MESH = pl.DeviceIdType.MESH


def dot(a, b, contract=((1,), (0,))):
    return lax.dot_general(a, b, (contract, ((), ())), preferred_element_type=f32)


def dot_nt(a, b):
    return dot(a, b, ((1,), (1,)))


def dot_tn(a, b):
    return dot(a, b, ((0,), (0,)))


def iota(shape, dim):
    return lax.broadcasted_iota(jnp.int32, shape, dim).astype(f32)


def whole(x, unit):
    return jnp.floor((x + 0.5) * (1.0 / unit))


def one_hot(condition):
    return jnp.where(condition, 1.0, 0.0).astype(bf16)


def each(first, last, step):
    if last - first <= 16:
        for k in range(first, last):
            step(k)
    else:
        pl.loop(first, last)(step)


def kernel(
    rows,
    cols,
    pair,
    gain_ref,
    bw,
    single,
    wq,
    wk,
    wv,
    wo,
    mask_ref,
    og,
    pair_grad,
    single_grad,
    wgq,
    wgk,
    wgv,
    wgo,
    bwg,
    gg,
    sbuf,
    gbuf,
    stat,
    a_send,
    a_recv,
    q_send,
    q_recv,
    kv_send,
    kv_recv,
    ag,
    fin,
    normed,
    inv,
    ebuf,
    gpbuf,
    plow,
    glow,
    qd,
    gd,
    hm,
    stat_rows,
    att_acc,
    qg_acc,
    kg_acc,
    vg_acc,
    bw_acc,
    gain_acc,
    sems,
    stat_sems,
    a_sems,
    q_sems,
    kv_sems,
):
    group = rows * cols
    own, width = single.shape
    padded = sbuf.shape[1]
    row_count, col_count, channels = pair.shape
    row = lax.axis_index("row")
    col = lax.axis_index("col")
    me = row * cols + col
    scale = HEAD ** (-0.5)
    chunk = 16 if row_count % 16 == 0 else 8 if row_count % 8 == 0 else row_count
    crows = chunk * HEADS
    pad_rows = cols * padded
    pad_cols = rows * padded

    def device(index):
        return {"row": index // cols, "col": index % cols}

    def peer(k):
        return lax.rem(me + k, group)

    def sender(k):
        return lax.rem(me + group - k, group)

    barrier = pltpu.get_barrier_semaphore()

    def greet(k):
        pl.semaphore_signal(barrier, inc=1, device_id=device(peer(k)), device_id_type=MESH)

    each(1, group, greet)

    def gather(buf, kind):
        def copy(k, slot):
            return pltpu.make_async_remote_copy(
                src_ref=buf.at[me],
                dst_ref=buf.at[slot],
                send_sem=sems.at[2 * kind, k],
                recv_sem=sems.at[2 * kind + 1, k],
                device_id=device(peer(k)),
                device_id_type=MESH,
            )

        return (
            lambda: each(1, group, lambda k: copy(k, me).start()),
            lambda: each(1, group, lambda k: copy(k, sender(k)).wait_recv()),
            lambda: each(1, group, lambda k: copy(k, me).wait_send()),
        )

    def along_col(src_of, buf, col_sems):
        def copy(k, slot):
            target = lax.rem(col + k, cols)
            return pltpu.make_async_remote_copy(
                src_ref=src_of(target),
                dst_ref=buf.at[slot],
                send_sem=col_sems.at[0, k],
                recv_sem=col_sems.at[1, k],
                device_id={"row": row, "col": target},
                device_id_type=MESH,
            )

        return (
            lambda: each(1, cols, lambda k: copy(k, col).start()),
            lambda: each(
                1, cols, lambda k: copy(k, lax.rem(col + cols - k, cols)).wait_recv()
            ),
            lambda: each(1, cols, lambda k: copy(k, col).wait_send()),
        )

    s_start, s_recv, s_sent = gather(sbuf, 0)
    g_start, g_recv, g_sent = gather(gbuf, 1)
    ag_start, ag_recv, ag_sent = gather(ag, 2)
    fin_start, fin_recv, fin_sent = gather(fin, 3)
    st_start, st_recv, st_sent = along_col(lambda target: stat.at[col], stat, stat_sems)
    a_start, a_wait, a_sent = along_col(lambda target: a_send.at[target], a_recv, a_sems)
    q_start, q_wait, q_sent = along_col(lambda target: q_send.at[target], q_recv, q_sems)

    pad_own = one_hot(iota((padded, own), 0) == iota((padded, own), 1))
    sbuf[me] = dot(pad_own, single[...]).astype(bf16)
    gbuf[me] = dot(pad_own, og[...]).astype(bf16)
    pl.semaphore_wait(barrier, group - 1)
    s_start()
    g_start()

    gain = gain_ref[...]
    eye = one_hot(iota((HEADS, HEADS), 0) == iota((HEADS, HEADS), 1))
    bw_t = dot_nt(eye, bw[...]).astype(bf16)

    def forward_row(i):
        x = pair[i].astype(f32)
        centred = x - jnp.mean(x, axis=1, keepdims=True)
        inverse = lax.rsqrt(jnp.mean(centred * centred, axis=1, keepdims=True) + norm_eps)
        norm = centred * inverse
        normed[i] = norm
        inv[i] = inverse
        ebuf[pl.ds(pl.multiple_of(i * HEADS, HEADS), HEADS), :] = dot_nt(
            bw_t, (norm * gain).astype(bf16)
        )

    unroll = 8 if row_count % 8 == 0 else 1

    @pl.loop(0, row_count // unroll)
    def _(block):
        for u in range(unroll):
            forward_row(block * unroll + u)

    line = iota((crows, 1), 0)
    line_query = whole(line, HEADS)
    line_head = line - line_query * HEADS
    hm[...] = jnp.where(whole(iota((1, width), 1), HEAD) == line_head, 1.0, 0.0)
    lane_gap = iota((1, 128), 1) - line_head
    slot_of = iota((1, pad_rows), 1)
    slot_in = slot_of - whole(slot_of, padded) * padded
    slot_token = jnp.where(slot_in < own, whole(slot_of, padded) * own + slot_in, -1.0)
    slot_of_t = iota((pad_rows, 1), 0)
    slot_in_t = slot_of_t - whole(slot_of_t, padded) * padded
    slot_token_t = jnp.where(
        slot_in_t < own, whole(slot_of_t, padded) * own + slot_in_t, -1.0
    )
    line_query_t = whole(iota((1, crows), 1), HEADS)
    key_slot = iota((1, pad_cols), 1)
    key_in = key_slot - whole(key_slot, padded) * padded
    key_token = jnp.where(key_in < own, whole(key_slot, padded) * own + key_in, -1.0)
    key_slot_t = iota((pad_cols, 1), 0)
    key_in_t = key_slot_t - whole(key_slot_t, padded) * padded
    key_token_t = jnp.where(key_in_t < own, whole(key_slot_t, padded) * own + key_in_t, -1.0)
    pick_keys = one_hot(key_token == iota((col_count, 1), 0))
    pick_keys_t = one_hot(key_token_t == iota((1, col_count), 1))

    s_recv()
    row_tokens = sbuf[pl.ds(row * cols, cols)].reshape(pad_rows, width)
    col_tokens = sbuf[pl.ds(col * rows, rows)].reshape(pad_cols, width)
    query = dot(row_tokens, wq[...]).astype(bf16)
    key = dot(pick_keys, dot(col_tokens, wk[...]).astype(bf16)).astype(bf16)
    value = dot(pick_keys, dot(col_tokens, wv[...]).astype(bf16)).astype(bf16)
    g_recv()
    grad_tokens = gbuf[pl.ds(row * cols, cols)].reshape(pad_rows, width)
    grad_att = dot_nt(grad_tokens, wo[...]).astype(bf16)
    live = mask_ref[...] > 0

    @pl.loop(0, row_count // chunk)
    def _(block):
        lines = pl.ds(pl.multiple_of(block * crows, crows), crows)
        first = (block * chunk).astype(f32)
        spread = one_hot(slot_token == line_query + first)
        q_diag = (dot(spread, query) * hm[...]).astype(bf16)
        g_diag = (dot(spread, grad_att) * hm[...]).astype(bf16)
        qd[lines, :] = q_diag
        gd[lines, :] = g_diag
        scores = dot_nt(q_diag, key) * scale + ebuf[lines, :]
        scores = jnp.where(live, scores, masked_score)
        top = jnp.max(scores, axis=1, keepdims=True)
        exps = jnp.exp(scores - top)
        grad_probs = dot_nt(g_diag, value)
        total = jnp.sum(exps, axis=1, keepdims=True)
        part = jnp.sum(exps * grad_probs, axis=1, keepdims=True)
        ebuf[lines, :] = exps
        gpbuf[lines, :] = grad_probs
        placed = jnp.where(
            lane_gap == 0.0,
            top,
            jnp.where(
                lane_gap == float(HEADS), total, jnp.where(lane_gap == 2.0 * HEADS, part, 0.0)
            ),
        )
        stat_rows[pl.ds(pl.multiple_of(block * chunk, chunk), chunk), :] = jnp.sum(
            placed.reshape(chunk, HEADS, 128), axis=1
        )

    stat[col] = stat_rows[...].T[: 3 * HEADS]
    st_start()
    st_recv()
    own_top = stat[col, 0:HEADS]
    row_top = stat[0, 0:HEADS]
    for k in range(1, cols):
        row_top = jnp.maximum(row_top, stat[k, 0:HEADS])
    row_total = jnp.zeros_like(row_top)
    delta = jnp.zeros_like(row_top)
    for k in range(cols):
        weight = jnp.exp(stat[k, 0:HEADS] - row_top)
        row_total += weight * stat[k, HEADS : 2 * HEADS]
        delta += weight * stat[k, 2 * HEADS : 3 * HEADS]
    factor = jnp.exp(own_top - row_top) / row_total
    delta = delta / row_total
    stat_rows[...] = jnp.concatenate(
        [factor, delta, jnp.zeros((128 - 2 * HEADS, row_count), f32)], axis=0
    ).T

    att_acc[...] = jnp.zeros_like(att_acc)
    qg_acc[...] = jnp.zeros_like(qg_acc)
    kg_acc[...] = jnp.zeros_like(kg_acc)
    vg_acc[...] = jnp.zeros_like(vg_acc)

    @pl.loop(0, row_count // chunk)
    def _(block):
        lines = pl.ds(pl.multiple_of(block * crows, crows), crows)
        first = (block * chunk).astype(f32)
        stats = stat_rows[pl.ds(pl.multiple_of(block * chunk, chunk), chunk), :]
        stats = jnp.broadcast_to(stats[:, None, :], (chunk, HEADS, 128)).reshape(crows, 128)
        factor = jnp.sum(jnp.where(lane_gap == 0.0, stats, 0.0), axis=1, keepdims=True)
        delta = jnp.sum(jnp.where(lane_gap == float(HEADS), stats, 0.0), axis=1, keepdims=True)
        probs = ebuf[lines, :] * factor
        probs_low = probs.astype(bf16)
        grad_low = (probs * (gpbuf[lines, :] - delta)).astype(bf16)
        glow[lines, :] = grad_low
        fold = one_hot(slot_token_t == line_query_t + first)
        att = (dot(probs_low, value) * hm[...]).astype(bf16)
        att_acc[...] += dot(fold, att)
        query_grad = (dot(grad_low, key) * (scale * hm[...])).astype(bf16)
        qg_acc[...] += dot(fold, query_grad)
        kg_acc[...] += dot_tn(grad_low, qd[lines, :])
        vg_acc[...] += dot_tn(probs_low, gd[lines, :])

    a_send[...] = att_acc[...].reshape(cols, padded, width).astype(bf16)
    q_send[...] = qg_acc[...].reshape(cols, padded, width).astype(bf16)
    key_side = dot(pick_keys_t, (kg_acc[...] * scale).astype(bf16))
    value_side = dot(pick_keys_t, vg_acc[...].astype(bf16))
    kv_send[:, 0] = key_side.reshape(rows, padded, width).astype(bf16)
    kv_send[:, 1] = value_side.reshape(rows, padded, width).astype(bf16)

    def kv_copy(b, slot):
        return pltpu.make_async_remote_copy(
            src_ref=kv_send.at[b],
            dst_ref=kv_recv.at[slot],
            send_sem=kv_sems.at[0, b],
            recv_sem=kv_sems.at[1, slot],
            device_id=device(col * rows + b),
            device_id_type=MESH,
        )

    def kv_start(b):
        pl.when(col * rows + b != me)(lambda: kv_copy(b, row).start())

    def kv_sent(b):
        pl.when(col * rows + b != me)(lambda: kv_copy(b, row).wait_send())

    def kv_wait(r):
        pl.when(r * cols + me // rows != me)(lambda: kv_copy(0, r).wait_recv())

    each(0, rows, kv_start)
    q_start()
    a_start()
    a_recv[col] = a_send[col]
    q_recv[col] = q_send[col]

    @pl.when(me // rows == col)
    def _():
        kv_recv[row] = kv_send[me % rows]

    bw_acc[...] = jnp.zeros_like(bw_acc)
    gain_acc[...] = jnp.zeros_like(gain_acc)

    def backward_row(i):
        grad_low = glow[pl.ds(pl.multiple_of(i * HEADS, HEADS), HEADS), :]
        norm = normed[i]
        grad_normed = dot_tn(grad_low, bw_t)
        bw_part = dot(grad_low, (norm * gain).astype(bf16))
        scaled = grad_normed * gain
        gain_part = grad_normed * norm
        along = jnp.mean(gain_part * gain, axis=1, keepdims=True)
        pair_grad[i] = (
            inv[i] * (scaled - jnp.mean(scaled, axis=1, keepdims=True) - norm * along)
        ).astype(bf16)
        return bw_part, gain_part

    def backward(first, last):
        @pl.loop(first // unroll, last // unroll)
        def _(block):
            bw_sum = bw_acc[...]
            gain_sum = gain_acc[...]
            for u in range(unroll):
                bw_part, gain_part = backward_row(block * unroll + u)
                bw_sum += bw_part
                gain_sum += gain_part
            bw_acc[...] = bw_sum
            gain_acc[...] = gain_sum

    split = (row_count // unroll // 2) * unroll
    backward(0, split)

    a_wait()
    q_wait()
    each(0, rows, kv_wait)
    att_own = a_recv[0].astype(f32)
    qg_own = q_recv[0].astype(f32)
    for k in range(1, cols):
        att_own += a_recv[k].astype(f32)
        qg_own += q_recv[k].astype(f32)
    kg_own = kv_recv[0, 0].astype(f32)
    vg_own = kv_recv[0, 1].astype(f32)
    for k in range(1, rows):
        kg_own += kv_recv[k, 0].astype(f32)
        vg_own += kv_recv[k, 1].astype(f32)
    qg_low = qg_own.astype(bf16)
    kg_low = kg_own.astype(bf16)
    vg_low = vg_own.astype(bf16)
    ag[me, 0] = qg_low
    ag[me, 1] = kg_low
    ag[me, 2] = vg_low
    ag[me, 3] = att_own.astype(bf16)
    ag_start()

    backward(split, row_count)
    fin[me, 0:HEADS] = bw_acc[...]
    fin[me, HEADS : HEADS + 8] = jnp.broadcast_to(
        jnp.sum(gain_acc[...], axis=0, keepdims=True), (8, channels)
    )
    fin_start()
    out_rows = dot_nt(qg_low, wq[...]) + dot_nt(kg_low, wk[...]) + dot_nt(vg_low, wv[...])
    single_grad[...] = out_rows[:own].astype(bf16)

    share = wgq.shape[0]
    share_pad = (share + 15) // 16 * 16
    pick = one_hot(
        iota((share_pad, width), 1)
        == iota((share_pad, width), 0) + (me * share).astype(f32)
    )
    tokens_t = dot_nt(pick, sbuf[...].reshape(group * padded, width)).astype(bf16)
    ag_recv()
    for k, out in enumerate((wgq, wgk, wgv)):
        out[...] = dot(tokens_t, ag[:, k].reshape(group * padded, width))[:share]
    att_t = dot_nt(pick, ag[:, 3].reshape(group * padded, width)).astype(bf16)
    wgo[...] = dot(att_t, gbuf[...].reshape(group * padded, width))[:share]

    fin_recv()
    total_parts = fin[0]
    for k in range(1, group):
        total_parts += fin[k]
    bwg[...] = total_parts[0:HEADS].T
    gg[...] = total_parts[HEADS : HEADS + 1]
    s_sent()
    g_sent()
    st_sent()
    a_sent()
    q_sent()
    each(0, rows, kv_sent)
    ag_sent()
    fin_sent()


def body(rows, cols, pair, pair_gain, bias_weight, single, w_query, w_key, w_value, w_out, key_mask, out_grad):
    row_count, col_count, channels = pair.shape
    own, width = single.shape
    group = rows * cols
    padded = (own + 15) // 16 * 16
    lines = row_count * HEADS
    share = width // group
    chunk = 16 if row_count % 16 == 0 else 8 if row_count % 8 == 0 else row_count
    vmem = pl.BlockSpec(memory_space=pltpu.VMEM)
    shape = jax.ShapeDtypeStruct
    outs = pl.pallas_call(
        functools.partial(kernel, rows, cols),
        out_shape=(
            shape(pair.shape, bf16),
            shape(single.shape, bf16),
            shape((share, width), f32),
            shape((share, width), f32),
            shape((share, width), f32),
            shape((share, width), f32),
            shape((channels, HEADS), f32),
            shape((1, channels), f32),
        ),
        in_specs=[vmem] * 10,
        out_specs=(vmem,) * 8,
        scratch_shapes=[
            pltpu.VMEM((group, padded, width), bf16),
            pltpu.VMEM((group, padded, width), bf16),
            pltpu.VMEM((cols, 3 * HEADS, row_count), f32),
            pltpu.VMEM((cols, padded, width), bf16),
            pltpu.VMEM((cols, padded, width), bf16),
            pltpu.VMEM((cols, padded, width), bf16),
            pltpu.VMEM((cols, padded, width), bf16),
            pltpu.VMEM((rows, 2, padded, width), bf16),
            pltpu.VMEM((rows, 2, padded, width), bf16),
            pltpu.VMEM((group, 4, padded, width), bf16),
            pltpu.VMEM((group, HEADS + 8, channels), f32),
            pltpu.VMEM((row_count, col_count, channels), f32),
            pltpu.VMEM((row_count, col_count, 1), f32),
            pltpu.VMEM((lines, col_count), f32),
            pltpu.VMEM((lines, col_count), f32),
            pltpu.VMEM((16, 128), bf16),
            pltpu.VMEM((lines, col_count), bf16),
            pltpu.VMEM((lines, width), bf16),
            pltpu.VMEM((lines, width), bf16),
            pltpu.VMEM((chunk * HEADS, width), f32),
            pltpu.VMEM((row_count, 128), f32),
            pltpu.VMEM((cols * padded, width), f32),
            pltpu.VMEM((cols * padded, width), f32),
            pltpu.VMEM((col_count, width), f32),
            pltpu.VMEM((col_count, width), f32),
            pltpu.VMEM((HEADS, channels), f32),
            pltpu.VMEM((col_count, channels), f32),
            pltpu.SemaphoreType.DMA((8, group)),
            pltpu.SemaphoreType.DMA((2, cols)),
            pltpu.SemaphoreType.DMA((2, cols)),
            pltpu.SemaphoreType.DMA((2, cols)),
            pltpu.SemaphoreType.DMA((2, rows)),
        ],
        compiler_params=pltpu.CompilerParams(
            collective_id=0, has_side_effects=True, vmem_limit_bytes=50 * 1024 * 1024
        ),
    )(
        pair,
        pair_gain.reshape(1, channels),
        bias_weight,
        single,
        w_query,
        w_key,
        w_value,
        w_out,
        key_mask.reshape(1, col_count),
        out_grad,
    )
    return outs[:-1] + (outs[-1].reshape(channels),)


def solution(mesh):
    tokens = ("sample", "row", "col")
    in_specs = (
        P(("sample", "row"), "col", None),
        P(),
        P(),
        P(tokens, None),
        P(),
        P(),
        P(),
        P(),
        P(("sample", "col")),
        P(tokens, None),
    )
    out_specs = (
        P(("sample", "row"), "col", None),
        P(tokens, None),
        P(tokens, None),
        P(tokens, None),
        P(tokens, None),
        P(tokens, None),
        P("sample", None),
        P("sample"),
    )
    return jax.shard_map(
        functools.partial(body, mesh.shape["row"], mesh.shape["col"]),
        mesh=mesh,
        in_specs=in_specs,
        out_specs=out_specs,
        check_vma=False,
    )
```

time: 232 us -> 71.9 us (0.31)
  blocking collectives: 98.1 us -> 0 us
  waiting for transfers between devices: 69.6 us -> 0 us
  Pallas kernels: 0 us -> 57.9 us
  matrix products: 24.6 us -> 0 us
  between operations: 16.8 us -> 0.66 us
  other arithmetic: 12.5 us -> 0 us
  local copies, waits for them, and re-layouts: 6.04 us -> 12.9 us
  starting transfers between devices: 4.23 us -> 0 us
    pallas_call x0 -> x1, Pallas kernels: none -> 57.9 us  [body(): pl.pallas_call(functools.partial(kernel, rows, cols), out_shape=(shape(pa...]
    reduce_scatter x4 -> x0, waiting for transfers between devices: 50.7 us -> none  [the longest x1 35.5 us: body(): lax.psum_scatter(out_terms, ('row', 'col'), scatter_dimension=0, tiled=True)]
    all_gather x2 -> x0, blocking collectives: 39.7 us -> none  [the longest x1 26.3 us: body(): all_single = lax.all_gather(single, ('row', 'col'), axis=0, tiled=True)]
    psum x2 -> x0, blocking collectives: 25 us -> none  [the longest x1 16.5 us: body(): lax.psum((bias_grad_part, gain_grad_part), ('row', 'col'))]
    dot_general x20 -> x0, matrix products: 24.6 us -> none  [the longest x1 5.25 us: body(): jnp.einsum('hij,ch->ijc', grad_low, bias_weight, preferred_element_type=f32)]
    unnamed x1 -> x0, blocking collectives: 21.5 us -> none
    psum x1 -> x0, waiting for transfers between devices: 18.8 us -> none  [body(): attended = lax.psum(attended_part, 'col')]
    pmax x1 -> x0, blocking collectives: 11.8 us -> none  [body(): row_top = lax.pmax(local_top, 'col')]
  transfers between devices with their start and end apart: 6 -> 0, of which waited for: 3 -> 0; matrix products, arithmetic and copies ran while one was open for 21% -> 0% of each run, Pallas kernels for 0% -> 0%
where the time goes in v1:
time: 71.9 us; the launch traced here: 71.4 us
  Pallas kernels  57.9 us (81%)
  local copies, waits for them, and re-layouts  12.9 us (18%)
    pallas_call x1, Pallas kernels, body(): pl.pallas_call(functools.partial(kernel, rows, cols), out_shape=(shape(pa...  57.9 us
    unnamed x25, local copies, waits for them, and re-layouts  12.9 us

profile of v1, /device:TPU:0, one launch (start us, length us, event | category | flops | bytes accessed | tf_op | source)
XLA Modules:
  0.0 71.4 jit_solution(15367149496228115191)
XLA Ops:
  0.6 0.8 %copy.18.bw = bf16[128,16]{1,0:T(8,128)(2,1)S(1)} copy(bf16[128,16]{0,1:T(8,128)(2,1)} %param.12) | data formatting | bytes 8192 | tf_op args[2]
  1.4 0.0 copy-start
  1.4 1.0 %copy-done = bf16[384,384]{1,0:T(8,128)(2,1)S(1)} copy-done((bf16[384,384]{1,0:T(8,128)(2,1)S(1)}, bf16[384,384]{1,0:T(8,128)(2,1)}, u32[]{:S(2)}) %copy-start) | copy-done | bytes 294936
  2.4 0.0 copy-start.1
  2.4 1.0 %copy-done.1 = bf16[384,384]{1,0:T(8,128)(2,1)S(1)} copy-done((bf16[384,384]{1,0:T(8,128)(2,1)S(1)}, bf16[384,384]{1,0:T(8,128)(2,1)}, u32[]{:S(2)}) %copy-start.1) | copy-done | bytes 294936
  3.4 0.0 copy-start.2
  3.4 1.0 %copy-done.2 = bf16[384,384]{1,0:T(8,128)(2,1)S(1)} copy-done((bf16[384,384]{1,0:T(8,128)(2,1)S(1)}, bf16[384,384]{1,0:T(8,128)(2,1)}, u32[]{:S(2)}) %copy-start.2) | copy-done | bytes 294936
  4.3 0.0 copy-start.3
  4.3 1.0 %copy-done.3 = bf16[384,384]{1,0:T(8,128)(2,1)S(1)} copy-done((bf16[384,384]{1,0:T(8,128)(2,1)S(1)}, bf16[384,384]{1,0:T(8,128)(2,1)}, u32[]{:S(2)}) %copy-start.3) | copy-done | bytes 294936
  5.3 0.0 copy-start.4
  5.3 0.7 %copy-done.4 = bf16[28,384]{1,0:T(8,128)(2,1)S(1)} copy-done((bf16[28,384]{1,0:T(8,128)(2,1)S(1)}, bf16[28,384]{1,0:T(8,128)(2,1)}, u32[]{:S(2)}) %copy-start.4) | copy-done | bytes 21528
  6.0 0.0 copy-start.5
  6.0 0.7 %copy-done.5 = bf16[28,384]{1,0:T(8,128)(2,1)S(1)} copy-done((bf16[28,384]{1,0:T(8,128)(2,1)S(1)}, bf16[28,384]{1,0:T(8,128)(2,1)}, u32[]{:S(2)}) %copy-start.5) | copy-done | bytes 21528
  6.8 0.0 copy-start.6
  6.8 0.7 copy-done.6
  7.4 0.0 copy-start.7
  7.4 0.7 copy-done.7
  8.1 57.9 %shard_map.161 = (bf16[112,56,128]{2,1,0:T(8,128)(2,1)S(1)}, bf16[28,384]{1,0:T(8,128)(2,1)S(1)}, f32[48,384]{1,0:T(8,128)S(1)}, f32[48,384]{1,0:T(8,128)S(1)}, ...) custom-call(bf16[112,56,128]{2,1,0:T(8,128)(2,1)} %pair.1, ...), custom_call_target="tpu_custom_call" | custom-call | tf_op jit(solution)/shard_map/pallas_call | solution.py:453
  65.9 0.7 copy.19
  66.6 1.2 %copy.27 = bf16[112,56,128]{2,1,0:T(8,128)(2,1)} copy(bf16[112,56,128]{2,1,0:T(8,128)(2,1)S(1)} %get-tuple-element.40) | data formatting | bytes 3211264
  67.8 0.6 copy.28
  68.4 0.6 copy.29
  69.0 0.6 copy.30
  69.6 0.6 copy.31
  70.3 0.6 copy.32
  70.9 0.5 copy.33
Async XLA Ops:
  1.4 1.0 %copy-start = (bf16[384,384]{1,0:T(8,128)(2,1)S(1)}, bf16[384,384]{1,0:T(8,128)(2,1)}, u32[]{:S(2)}) copy-start(bf16[384,384]{1,0:T(8,128)(2,1)} %wq.1) | copy-start | bytes 884740
  2.4 1.0 %copy-start.1 = (bf16[384,384]{1,0:T(8,128)(2,1)S(1)}, bf16[384,384]{1,0:T(8,128)(2,1)}, u32[]{:S(2)}) copy-start(bf16[384,384]{1,0:T(8,128)(2,1)} %wk.1) | copy-start | bytes 884740
  3.4 1.0 %copy-start.2 = (bf16[384,384]{1,0:T(8,128)(2,1)S(1)}, bf16[384,384]{1,0:T(8,128)(2,1)}, u32[]{:S(2)}) copy-start(bf16[384,384]{1,0:T(8,128)(2,1)} %wv.1) | copy-start | bytes 884740
  4.3 1.0 %copy-start.3 = (bf16[384,384]{1,0:T(8,128)(2,1)S(1)}, bf16[384,384]{1,0:T(8,128)(2,1)}, u32[]{:S(2)}) copy-start(bf16[384,384]{1,0:T(8,128)(2,1)} %wo.1) | copy-start | bytes 884740
  5.3 0.7 %copy-start.4 = (bf16[28,384]{1,0:T(8,128)(2,1)S(1)}, bf16[28,384]{1,0:T(8,128)(2,1)}, u32[]{:S(2)}) copy-start(bf16[28,384]{1,0:T(8,128)(2,1)} %single.1) | copy-start | bytes 64516
  6.0 0.7 %copy-start.5 = (bf16[28,384]{1,0:T(8,128)(2,1)S(1)}, bf16[28,384]{1,0:T(8,128)(2,1)}, u32[]{:S(2)}) copy-start(bf16[28,384]{1,0:T(8,128)(2,1)} %og.1) | copy-start | bytes 64516
  6.8 0.7 copy-start.6
  7.4 0.7 copy-start.7

commit v2 on v1

--- a/solution.py
+++ b/solution.py
@@ -52,16 +52,16 @@
 def kernel(
     rows,
     cols,
-    pair,
-    gain_ref,
-    bw,
-    single,
-    wq,
-    wk,
-    wv,
-    wo,
-    mask_ref,
-    og,
+    pair_hbm,
+    gain_hbm,
+    bw_hbm,
+    single_hbm,
+    wq_hbm,
+    wk_hbm,
+    wv_hbm,
+    wo_hbm,
+    mask_hbm,
+    og_hbm,
     pair_grad,
     single_grad,
     wgq,
@@ -102,6 +102,23 @@
     a_sems,
     q_sems,
     kv_sems,
+    s_sems,
+    g_sems,
+    ag_sems,
+    s_row_sems,
+    g_row_sems,
+    ag_row_sems,
+    pair,
+    gain_ref,
+    bw,
+    single,
+    wq,
+    wk,
+    wv,
+    wo,
+    mask_ref,
+    og,
+    in_sems,
 ):
     group = rows * cols
     own, width = single.shape
@@ -125,15 +142,34 @@
     def sender(k):
         return lax.rem(me + group - k, group)
 
+    loads = [
+        pltpu.make_async_copy(source, target, in_sems.at[k])
+        for k, (source, target) in enumerate(
+            (
+                (single_hbm, single),
+                (og_hbm, og),
+                (gain_hbm, gain_ref),
+                (bw_hbm, bw),
+                (pair_hbm, pair),
+                (wq_hbm, wq),
+                (wk_hbm, wk),
+                (wv_hbm, wv),
+                (wo_hbm, wo),
+                (mask_hbm, mask_ref),
+            )
+        )
+    ]
     barrier = pltpu.get_barrier_semaphore()
 
     def greet(k):
         pl.semaphore_signal(barrier, inc=1, device_id=device(peer(k)), device_id_type=MESH)
 
     each(1, group, greet)
+    for load in loads:
+        load.start()
 
     def gather(buf, kind):
-        def copy(k, slot):
+        def direct(k, slot):
             return pltpu.make_async_remote_copy(
                 src_ref=buf.at[me],
                 dst_ref=buf.at[slot],
@@ -144,10 +180,56 @@
             )
 
         return (
-            lambda: each(1, group, lambda k: copy(k, me).start()),
-            lambda: each(1, group, lambda k: copy(k, sender(k)).wait_recv()),
-            lambda: each(1, group, lambda k: copy(k, me).wait_send()),
+            lambda: each(1, group, lambda k: direct(k, me).start()),
+            lambda: each(1, group, lambda k: direct(k, sender(k)).wait_recv()),
+            lambda: each(1, group, lambda k: direct(k, me).wait_send()),
         )
+
+    def gather_two(buf, col_sems, row_sems):
+        def across(k, slot):
+            return pltpu.make_async_remote_copy(
+                src_ref=buf.at[me],
+                dst_ref=buf.at[slot],
+                send_sem=col_sems.at[0, k],
+                recv_sem=col_sems.at[1, k],
+                device_id={"row": row, "col": lax.rem(col + k, cols)},
+                device_id_type=MESH,
+            )
+
+        def relay(j, k, slot_row):
+            place = lax.rem(col + cols - k, cols)
+            return pltpu.make_async_remote_copy(
+                src_ref=buf.at[row * cols + place],
+                dst_ref=buf.at[slot_row * cols + place],
+                send_sem=row_sems.at[0, j, k],
+                recv_sem=row_sems.at[1, j, k],
+                device_id={"row": lax.rem(row + j, rows), "col": col},
+                device_id_type=MESH,
+            )
+
+        def start():
+            each(1, cols, lambda k: across(k, me).start())
+            each(1, rows, lambda j: relay(j, 0, row).start())
+
+        def pass_on():
+            def one(k):
+                across(k, row * cols + lax.rem(col + cols - k, cols)).wait_recv()
+                each(1, rows, lambda j: relay(j, k, row).start())
+
+            each(1, cols, one)
+
+        def receive():
+            def one(j):
+                slot_row = lax.rem(row + rows - j, rows)
+                each(0, cols, lambda k: relay(j, k, slot_row).wait_recv())
+
+            each(1, rows, one)
+
+        def sent():
+            each(1, cols, lambda k: across(k, me).wait_send())
+            each(1, rows, lambda j: each(0, cols, lambda k: relay(j, k, row).wait_send()))
+
+        return start, pass_on, receive, sent
 
     def along_col(src_of, buf, col_sems):
         def copy(k, slot):
@@ -169,14 +251,16 @@
             lambda: each(1, cols, lambda k: copy(k, col).wait_send()),
         )
 
-    s_start, s_recv, s_sent = gather(sbuf, 0)
-    g_start, g_recv, g_sent = gather(gbuf, 1)
-    ag_start, ag_recv, ag_sent = gather(ag, 2)
-    fin_start, fin_recv, fin_sent = gather(fin, 3)
+    s_start, s_pass, s_recv, s_sent = gather_two(sbuf, s_sems, s_row_sems)
+    g_start, g_pass, g_recv, g_sent = gather_two(gbuf, g_sems, g_row_sems)
+    ag_start, ag_pass, ag_recv, ag_sent = gather_two(ag, ag_sems, ag_row_sems)
+    fin_start, fin_recv, fin_sent = gather(fin, 0)
     st_start, st_recv, st_sent = along_col(lambda target: stat.at[col], stat, stat_sems)
     a_start, a_wait, a_sent = along_col(lambda target: a_send.at[target], a_recv, a_sems)
     q_start, q_wait, q_sent = along_col(lambda target: q_send.at[target], q_recv, q_sems)
 
+    loads[0].wait()
+    loads[1].wait()
     pad_own = one_hot(iota((padded, own), 0) == iota((padded, own), 1))
     sbuf[me] = dot(pad_own, single[...]).astype(bf16)
     gbuf[me] = dot(pad_own, og[...]).astype(bf16)
@@ -184,9 +268,10 @@
     s_start()
     g_start()
 
+    for load in loads[2:5]:
+        load.wait()
     gain = gain_ref[...]
-    eye = one_hot(iota((HEADS, HEADS), 0) == iota((HEADS, HEADS), 1))
-    bw_t = dot_nt(eye, bw[...]).astype(bf16)
+    bw_t = bw[...]
 
     def forward_row(i):
         x = pair[i].astype(f32)
@@ -229,13 +314,16 @@
     pick_keys = one_hot(key_token == iota((col_count, 1), 0))
     pick_keys_t = one_hot(key_token_t == iota((1, col_count), 1))
 
+    for load in loads[5:]:
+        load.wait()
+    s_pass()
     s_recv()
     row_tokens = sbuf[pl.ds(row * cols, cols)].reshape(pad_rows, width)
     col_tokens = sbuf[pl.ds(col * rows, rows)].reshape(pad_cols, width)
     query = dot(row_tokens, wq[...]).astype(bf16)
     key = dot(pick_keys, dot(col_tokens, wk[...]).astype(bf16)).astype(bf16)
     value = dot(pick_keys, dot(col_tokens, wv[...]).astype(bf16)).astype(bf16)
-    g_recv()
+    g_pass()
     grad_tokens = gbuf[pl.ds(row * cols, cols)].reshape(pad_rows, width)
     grad_att = dot_nt(grad_tokens, wo[...]).astype(bf16)
     live = mask_ref[...] > 0
@@ -418,6 +506,8 @@
         == iota((share_pad, width), 0) + (me * share).astype(f32)
     )
     tokens_t = dot_nt(pick, sbuf[...].reshape(group * padded, width)).astype(bf16)
+    g_recv()
+    ag_pass()
     ag_recv()
     for k, out in enumerate((wgq, wgk, wgv)):
         out[...] = dot(tokens_t, ag[:, k].reshape(group * padded, width))[:share]
@@ -428,7 +518,7 @@
     total_parts = fin[0]
     for k in range(1, group):
         total_parts += fin[k]
-    bwg[...] = total_parts[0:HEADS].T
+    bwg[...] = total_parts[0:HEADS]
     gg[...] = total_parts[HEADS : HEADS + 1]
     s_sent()
     g_sent()
@@ -440,6 +530,24 @@
     fin_sent()
 
 
+def store(*refs):
+    sources, targets, held = refs[:8], refs[8:16], refs[16:24]
+    load_sems, store_sems = refs[24:]
+    loads = [
+        pltpu.make_async_copy(sources[k], held[k], load_sems.at[k]) for k in range(8)
+    ]
+    stores = [
+        pltpu.make_async_copy(held[k], targets[k], store_sems.at[k]) for k in range(8)
+    ]
+    for load in loads:
+        load.start()
+    for load, copy in zip(loads, stores):
+        load.wait()
+        copy.start()
+    for copy in stores:
+        copy.wait()
+
+
 def body(rows, cols, pair, pair_gain, bias_weight, single, w_query, w_key, w_value, w_out, key_mask, out_grad):
     row_count, col_count, channels = pair.shape
     own, width = single.shape
@@ -449,6 +557,7 @@
     share = width // group
     chunk = 16 if row_count % 16 == 0 else 8 if row_count % 8 == 0 else row_count
     vmem = pl.BlockSpec(memory_space=pltpu.VMEM)
+    hbm = pl.BlockSpec(memory_space=pltpu.HBM)
     shape = jax.ShapeDtypeStruct
     outs = pl.pallas_call(
         functools.partial(kernel, rows, cols),
@@ -459,10 +568,10 @@
             shape((share, width), f32),
             shape((share, width), f32),
             shape((share, width), f32),
-            shape((channels, HEADS), f32),
+            shape((HEADS, channels), f32),
             shape((1, channels), f32),
         ),
-        in_specs=[vmem] * 10,
+        in_specs=[hbm] * 10,
         out_specs=(vmem,) * 8,
         scratch_shapes=[
             pltpu.VMEM((group, padded, width), bf16),
@@ -492,19 +601,36 @@
             pltpu.VMEM((col_count, width), f32),
             pltpu.VMEM((HEADS, channels), f32),
             pltpu.VMEM((col_count, channels), f32),
-            pltpu.SemaphoreType.DMA((8, group)),
+            pltpu.SemaphoreType.DMA((2, group)),
             pltpu.SemaphoreType.DMA((2, cols)),
             pltpu.SemaphoreType.DMA((2, cols)),
             pltpu.SemaphoreType.DMA((2, cols)),
             pltpu.SemaphoreType.DMA((2, rows)),
+            pltpu.SemaphoreType.DMA((2, cols)),
+            pltpu.SemaphoreType.DMA((2, cols)),
+            pltpu.SemaphoreType.DMA((2, cols)),
+            pltpu.SemaphoreType.DMA((2, rows, cols)),
+            pltpu.SemaphoreType.DMA((2, rows, cols)),
+            pltpu.SemaphoreType.DMA((2, rows, cols)),
+            pltpu.VMEM(pair.shape, bf16),
+            pltpu.VMEM((1, channels), f32),
+            pltpu.VMEM((HEADS, channels), bf16),
+            pltpu.VMEM(single.shape, bf16),
+            pltpu.VMEM(w_query.shape, bf16),
+            pltpu.VMEM(w_key.shape, bf16),
+            pltpu.VMEM(w_value.shape, bf16),
+            pltpu.VMEM(w_out.shape, bf16),
+            pltpu.VMEM((1, col_count), jnp.int32),
+            pltpu.VMEM(out_grad.shape, bf16),
+            pltpu.SemaphoreType.DMA((10,)),
         ],
         compiler_params=pltpu.CompilerParams(
-            collective_id=0, has_side_effects=True, vmem_limit_bytes=50 * 1024 * 1024
+            collective_id=0, has_side_effects=True, vmem_limit_bytes=64 * 1024 * 1024
         ),
     )(
         pair,
         pair_gain.reshape(1, channels),
-        bias_weight,
+        bias_weight.T,
         single,
         w_query,
         w_key,
@@ -513,7 +639,16 @@
         key_mask.reshape(1, col_count),
         out_grad,
     )
-    return outs[:-1] + (outs[-1].reshape(channels),)
+    outs = pl.pallas_call(
+        store,
+        out_shape=tuple(shape(out.shape, out.dtype) for out in outs),
+        in_specs=[pl.BlockSpec(memory_space=pl.ANY)] * 8,
+        out_specs=(hbm,) * 8,
+        scratch_shapes=[pltpu.VMEM(out.shape, out.dtype) for out in outs]
+        + [pltpu.SemaphoreType.DMA((8,)), pltpu.SemaphoreType.DMA((8,))],
+        compiler_params=pltpu.CompilerParams(vmem_limit_bytes=64 * 1024 * 1024),
+    )(*outs)
+    return outs[:-2] + (outs[-2].T, outs[-1].reshape(channels))
 
 
 def solution(mesh):

time: 71.9 us -> 50.7 us (0.71)
  local copies, waits for them, and re-layouts: 12.9 us -> 0 us
  Pallas kernels: 57.9 us -> 49.9 us
    unnamed x25 -> x0, local copies, waits for them, and re-layouts: 12.9 us -> none
    pallas_call x1, Pallas kernels: 57.9 us -> 47.1 us  [body(): pl.pallas_call(functools.partial(kernel, rows, cols), out_shape=(shape(pa...]
    pallas_call x0 -> x1, Pallas kernels: none -> 2.81 us  [body(): pl.pallas_call(store, out_shape=tuple((shape(out.shape, out.dtype) for ou...]
where the time goes in v2:
time: 50.7 us; the launch traced here: 50.5 us
  Pallas kernels  49.9 us (98%)
  between operations  0.64 us (1%)
    pallas_call x1, Pallas kernels, body(): pl.pallas_call(functools.partial(kernel, rows, cols), out_shape=(shape(pa...  47.1 us
    pallas_call x1, Pallas kernels, body(): pl.pallas_call(store, out_shape=tuple((shape(out.shape, out.dtype) for ou...  2.81 us

profile of v2, /device:TPU:0, one launch (start us, length us, event | category | flops | bytes accessed | tf_op | source)
XLA Modules:
  0.0 50.5 jit_solution(10884901559325790355)
XLA Ops:
  0.6 47.1 %shard_map.161 = (bf16[112,56,128]{2,1,0:T(8,128)(2,1)}, bf16[28,384]{1,0:T(8,128)(2,1)}, f32[48,384]{1,0:T(8,128)}, f32[48,384]{1,0:T(8,128)}, f32[48,384]{1,0:...) custom-call(bf16[112,56,128]{2,1,0:T(8,128)(2,1)} %pair_hbm.1, f32[1,128]{1,0:T(1,128)} %bitcast.6, ...), custom_call_target="tpu_custom_call" | custom-call | tf_op jit(solution)/shard_map/pallas_call | solution.py:562
  47.7 2.8 %shard_map.162 = (bf16[112,56,128]{2,1,0:T(8,128)(2,1)}, bf16[28,384]{1,0:T(8,128)(2,1)}, f32[48,384]{1,0:T(8,128)}, f32[48,384]{1,0:T(8,128)}, f32[48,384]{1,0:...) custom-call(bf16[112,56,128]{2,1,0:T(8,128)(2,1)} %get-tuple-element.24.refs_0_, ...), custom_call_target="tpu_custom_call" | custom-call | tf_op jit(solution)/shard_map/pallas_call | solution.py:642

commit v3 on v2

--- a/solution.py
+++ b/solution.py
@@ -85,7 +85,6 @@
     inv,
     ebuf,
     gpbuf,
-    plow,
     glow,
     qd,
     gd,
@@ -286,10 +285,17 @@
 
     unroll = 8 if row_count % 8 == 0 else 1
 
-    @pl.loop(0, row_count // unroll)
-    def _(block):
-        for u in range(unroll):
-            forward_row(block * unroll + u)
+    split = (row_count // unroll // 2) * unroll
+
+    def forward(first, last):
+        @pl.loop(first // unroll, last // unroll)
+        def _(block):
+            for u in range(unroll):
+                forward_row(block * unroll + u)
+
+    forward(0, split)
+    s_pass()
+    forward(split, row_count)
 
     line = iota((crows, 1), 0)
     line_query = whole(line, HEADS)
@@ -316,7 +322,6 @@
 
     for load in loads[5:]:
         load.wait()
-    s_pass()
     s_recv()
     row_tokens = sbuf[pl.ds(row * cols, cols)].reshape(pad_rows, width)
     col_tokens = sbuf[pl.ds(col * rows, rows)].reshape(pad_cols, width)
@@ -465,7 +470,6 @@
             bw_acc[...] = bw_sum
             gain_acc[...] = gain_sum
 
-    split = (row_count // unroll // 2) * unroll
     backward(0, split)
 
     a_wait()
@@ -589,7 +593,6 @@
             pltpu.VMEM((row_count, col_count, 1), f32),
             pltpu.VMEM((lines, col_count), f32),
             pltpu.VMEM((lines, col_count), f32),
-            pltpu.VMEM((16, 128), bf16),
             pltpu.VMEM((lines, col_count), bf16),
             pltpu.VMEM((lines, width), bf16),
             pltpu.VMEM((lines, width), bf16),

time: 50.7 us -> 48.9 us (0.964)
  Pallas kernels: 49.9 us -> 48.1 us
    pallas_call x1, Pallas kernels: 47.1 us -> 45.3 us  [body(): pl.pallas_call(functools.partial(kernel, rows, cols), out_shape=(shape(pa...]
where the time goes in v3:
time: 48.9 us; the launch traced here: 48.8 us
  Pallas kernels  48.1 us (98%)
  between operations  0.64 us (1%)
    pallas_call x1, Pallas kernels, body(): pl.pallas_call(functools.partial(kernel, rows, cols), out_shape=(shape(pa...  45.3 us
    pallas_call x1, Pallas kernels, body(): pl.pallas_call(store, out_shape=tuple((shape(out.shape, out.dtype) for ou...  2.81 us

profile of v3, /device:TPU:0, one launch (start us, length us, event | category | flops | bytes accessed | tf_op | source)
XLA Modules:
  0.0 48.8 jit_solution(2194121326974653308)
XLA Ops:
  0.6 45.3 %shard_map.161 = (bf16[112,56,128]{2,1,0:T(8,128)(2,1)}, bf16[28,384]{1,0:T(8,128)(2,1)}, f32[48,384]{1,0:T(8,128)}, f32[48,384]{1,0:T(8,128)}, f32[48,384]{1,0:...) custom-call(bf16[112,56,128]{2,1,0:T(8,128)(2,1)} %pair_hbm.1, f32[1,128]{1,0:T(1,128)} %bitcast.6, ...), custom_call_target="tpu_custom_call" | custom-call | tf_op jit(solution)/shard_map/pallas_call | solution.py:566
  45.9 2.8 %shard_map.162 = (bf16[112,56,128]{2,1,0:T(8,128)(2,1)}, bf16[28,384]{1,0:T(8,128)(2,1)}, f32[48,384]{1,0:T(8,128)}, f32[48,384]{1,0:T(8,128)}, f32[48,384]{1,0:...) custom-call(bf16[112,56,128]{2,1,0:T(8,128)(2,1)} %get-tuple-element.24.refs_0_, ...), custom_call_target="tpu_custom_call" | custom-call | tf_op jit(solution)/shard_map/pallas_call | solution.py:645
